TPU v7x, 512 devices: a whole 4x8x8 slice. The times are simulated.
512 devices in a mesh: row: 8 (over z), col: 16 (over y, core), depth: 4 (over x).
Axes of the slice: x: 4, y: 8, z: 8, core: 2. Of those that a mesh axis runs over, the one named last changes fastest.
Arguments:
- tokens: bfloat16 [4096, 8192], P(('row', 'col'), 'depth'), may hold values from -6 to 6
- gate_weight: bfloat16 [8192, 14336], P(('depth', 'row'), 'col'), may hold values from -0.0625 to 0.0625
- up_weight: bfloat16 [8192, 14336], P(('depth', 'row'), 'col'), may hold values from -0.0625 to 0.0625
- down_weight: bfloat16 [14336, 8192], P(('col', 'row'), 'depth'), may hold values from -0.125 to 0.125
- gate_keep: int32 [64, 112], replicated, may hold values from 0 to 1, as said below
- up_keep: int32 [64, 112], replicated, may hold values from 0 to 1, as said below
- down_keep: int32 [112, 64], replicated, may hold values from 0 to 1, as said below
Outputs:
- mixed: bfloat16 [4096, 8192], P(('row', 'col'), 'depth')
Inputs may be any that keep to these rules, and one draw needn't show every extreme that they name: `gate_keep`: 1 marks a kept block of the gate projection, 0 a dropped one. `up_keep`: 1 marks a kept block of the up projection, 0 a dropped one. `down_keep`: 1 marks a kept block of the down projection, 0 a dropped one.
All inputs are finite; a program needn't handle non-finite values.
Results may differ from a plain program's by a relative error of at most 0.005.
Values may be sent and summed in bfloat16 or wider, within the bound.
No kernel may reach another device: no remote copies, remote signals or barrier semaphores. Data moves between devices by JAX's collectives and lax.ppermute only.
A program may use at most 64 MiB of HBM per device.

v0:
```python
import jax
import jax.numpy as jnp
from jax import lax
from jax.sharding import PartitionSpec as P

BLOCK = 128


def keep_table(keep, row_start, col_start, row_count, col_count):
    keep_bits = keep.astype(jnp.bfloat16)
    row_ids = (row_start + jnp.arange(row_count, dtype=jnp.int32)) // BLOCK
    col_ids = (col_start + jnp.arange(col_count, dtype=jnp.int32)) // BLOCK
    pick_rows = (row_ids[:, None] == jnp.arange(keep.shape[0], dtype=jnp.int32)[None, :]).astype(
        jnp.bfloat16
    )
    pick_cols = (jnp.arange(keep.shape[1], dtype=jnp.int32)[:, None] == col_ids[None, :]).astype(
        jnp.bfloat16
    )
    inner = jnp.dot(keep_bits, pick_cols, preferred_element_type=jnp.float32).astype(jnp.bfloat16)
    return jnp.dot(pick_rows, inner, preferred_element_type=jnp.float32).astype(jnp.bfloat16)


def add_panel(token_block, piece):
    return jnp.dot(token_block, piece, preferred_element_type=jnp.float32)


def on_device(tokens, gate_weight, up_weight, down_weight, gate_keep, up_keep, down_keep):
    depth_pos = lax.axis_index("depth")
    row_pos = lax.axis_index("row")
    column_pos = lax.axis_index("col")
    row_total = lax.axis_size("row")
    feature_rows = gate_weight.shape[0]
    hidden_cols = gate_weight.shape[1]
    feature_start = (depth_pos * row_total + row_pos) * feature_rows
    hidden_start = column_pos * hidden_cols
    gate_masked = gate_weight * keep_table(
        gate_keep, feature_start, hidden_start, feature_rows, hidden_cols
    )
    up_masked = up_weight * keep_table(
        up_keep, feature_start, hidden_start, feature_rows, hidden_cols
    )
    down_rows_count = down_weight.shape[0]
    down_features = down_weight.shape[1]
    down_start = (column_pos * row_total + row_pos) * down_rows_count
    down_masked = down_weight * keep_table(
        down_keep, down_start, depth_pos * down_features, down_rows_count, down_features
    )
    token_block = lax.all_gather(tokens, "col", axis=0, tiled=True)

    def add_one(piece):
        return add_panel(token_block, piece)

    gate = add_one(lax.all_gather(gate_masked, "row", axis=0, tiled=True))
    up = add_one(lax.all_gather(up_masked, "row", axis=0, tiled=True))
    both = jnp.stack((gate, up), 0)
    total = lax.psum(both, "depth")
    hidden = (jax.nn.silu(total[0]) * total[1]).astype(jnp.bfloat16)
    down_block = lax.all_gather(down_masked, "row", axis=0, tiled=True)
    mixed = lax.psum_scatter(
        jnp.dot(hidden, down_block, preferred_element_type=jnp.float32),
        "col",
        scatter_dimension=0,
        tiled=True,
    )
    return mixed.astype(jnp.bfloat16)


def solution(mesh):
    placed = (
        P(("row", "col"), "depth"),
        P(("depth", "row"), "col"),
        P(("depth", "row"), "col"),
        P(("col", "row"), "depth"),
        P(),
        P(),
        P(),
    )
    return jax.shard_map(
        on_device, mesh=mesh, in_specs=placed, out_specs=P(("row", "col"), "depth"), check_vma=False
    )
```

profile of v0, /device:TPU:25, one launch (start us, length us, event | category | flops | bytes accessed | tf_op | source)
XLA Modules:
  0.0 393.9 jit_solution(8674119538249657588)
XLA Ops:
  6.5 0.7 all-gather.7.cloned.1.call-update
  7.3 0.0 all-gather.9.cloned.1.call-start
  7.4 2.3 fusion.4
  9.7 0.0 all-gather.9.cloned.1.call-update
  9.7 0.0 all-gather.5.cloned.1.call-start
  9.8 2.3 fusion.3
  12.1 0.0 all-gather.5.cloned.1.call-update
  12.1 0.0 all-gather.11.cloned.1.call-start
  12.2 1.4 fusion
  13.7 0.0 all-gather.11.cloned.1.call-update
  13.7 0.0 all-reduce.2.cloned.1.call-start
  13.7 42.2 %all-gather.7.cloned.1.call-done = bf16[512,2048]{1,0:T(8,128)(2,1)} async-done(((bf16[32,2048]{1,0:T(8,128)(2,1)}), bf16[512,2048]{1,0:T(8,128)(2,1)}) %all-gather.7.cloned.1.call-update) | async-done | bytes 2097168 | tf_op jit(solution)/shard_map/all_gather | solution.py:48
  55.9 54.2 %all-gather.9.cloned.1.call-done = bf16[2048,896]{1,0:T(8,128)(2,1)} async-done(((bf16[256,896]{1,0:T(8,128)(2,1)}), bf16[2048,896]{1,0:T(8,128)(2,1)}) %all-gather.9.cloned.1.call-update) | async-done | bytes 3670032 | tf_op jit(solution)/shard_map/all_gather | solution.py:54
  110.2 4.8 %convolution_bitcast_fusion = f32[1,512,896]{1,2,0:T(8,128)S(1)} fusion(bf16[2048,896]{1,0:T(8,128)(2,1)} %all-gather.9.cloned.1.call-done, bf16[512,2048]{1,0:T(8,128)(2,1)} %all-gather.7.cloned.1.call-done), kind=kOutput, calls=%fused_computation.8 | convolution fusion | flops 1879048192 | bytes 7602176 | tf_op jit(solution)/shard_map/dot_general | solution.py:24
  115.0 48.7 %all-gather.5.cloned.1.call-done = bf16[2048,896]{1,0:T(8,128)(2,1)} async-done(((bf16[256,896]{1,0:T(8,128)(2,1)}), bf16[2048,896]{1,0:T(8,128)(2,1)}) %all-gather.5.cloned.1.call-update) | async-done | bytes 3670032 | tf_op jit(solution)/shard_map/all_gather | solution.py:53
  163.7 4.8 %convolution_bitcast_fusion.1 = f32[1,512,896]{1,2,0:T(8,128)S(1)} fusion(bf16[2048,896]{1,0:T(8,128)(2,1)} %all-gather.5.cloned.1.call-done, bf16[512,2048]{1,0:T(8,128)(2,1)} %all-gather.7.cloned.1.call-done), kind=kOutput, calls=%fused_computation.9 | convolution fusion | flops 1879048192 | bytes 7602176 | tf_op jit(solution)/shard_map/dot_general | solution.py:24
  168.5 2.3 pad_maximum_fusion
  170.8 0.0 all-reduce.2.cloned.1.call-update
  170.9 0.0 reduce-scatter.2.cloned.1.call-start
  170.9 46.2 %all-gather.11.cloned.1.call-done = bf16[896,2048]{1,0:T(8,128)(2,1)} async-done(((bf16[112,2048]{1,0:T(8,128)(2,1)}), bf16[896,2048]{1,0:T(8,128)(2,1)}) %all-gather.11.cloned.1.call-update) | async-done | bytes 3670032 | tf_op jit(solution)/shard_map/all_gather | solution.py:58
  217.1 95.3 %all-reduce.2.cloned.1.call-done = f32[2,512,896]{1,2,0:T(8,128)} async-done(((f32[2,512,896]{1,2,0:T(8,128)}), f32[2,512,896]{1,2,0:T(8,128)}) %all-reduce.2.cloned.1.call-update) | async-done | bytes 3670032 | tf_op jit(solution)/shard_map/psum | solution.py:56
  312.4 7.7 %fusion.5 = f32[512,2048]{1,0:T(8,128)} fusion(bf16[896,2048]{1,0:T(8,128)(2,1)} %all-gather.11.cloned.1.call-done, f32[2,512,896]{1,2,0:T(8,128)} %all-reduce.2.cloned.1.call-done), kind=kOutput, calls=%fused_computation.16 | convolution fusion | flops 1881800704 | bytes 11534336 | tf_op jit(solution)/shard_map/dot_general | solution.py:60
  320.1 65.3 %reduce-scatter.2.cloned.1.call-done = f32[32,2048]{1,0:T(8,128)} async-done(((f32[512,2048]{1,0:T(8,128)}), f32[32,2048]{1,0:T(8,128)}) %reduce-scatter.2.cloned.1.call-update) | async-done | bytes 262160 | tf_op jit(solution)/shard_map/reduce_scatter | solution.py:59
  385.4 1.6 convert_element_type.52
  (10 shorter events, 0.1 us)
Async XLA Ops:
  6.5 5.7 %copy-start = (bf16[112,2048]{1,0:T(8,128)(2,1)S(1)}, bf16[112,2048]{1,0:T(8,128)(2,1)}, u32[]{:S(2)}) copy-start(bf16[112,2048]{1,0:T(8,128)(2,1)} %param.10) | copy-start | bytes 1376260
  6.5 5.7 %copy-start.1 = (s32[112,64]{0,1:T(8,128)S(1)}, s32[112,64]{0,1:T(8,128)}, u32[]{:S(2)}) copy-start(s32[112,64]{0,1:T(8,128)} %param.13) | copy-start | bytes 86020
  6.5 49.4 %all-gather.7.cloned.1.call-start = ((), (), s32[]{:S(2)}) async-start(), calls=%async_computation.2 | async-start | bytes 2228224 | tf_op jit(solution)/shard_map/all_gather | solution.py:48
  7.3 102.9 %all-gather.9.cloned.1.call-start = ((), (), s32[]{:S(2)}) async-start(), calls=%async_computation.3 | async-start | bytes 4128768 | tf_op jit(solution)/shard_map/all_gather | solution.py:54
  9.7 154.0 %all-gather.5.cloned.1.call-start = ((), (), s32[]{:S(2)}) async-start(), calls=%async_computation.1 | async-start | bytes 4128768 | tf_op jit(solution)/shard_map/all_gather | solution.py:53
  12.1 205.0 %all-gather.11.cloned.1.call-start = ((), (), s32[]{:S(2)}) async-start(), calls=%async_computation.5 | async-start | bytes 4128768 | tf_op jit(solution)/shard_map/all_gather | solution.py:58
  13.7 298.7 %all-reduce.2.cloned.1.call-start = ((), (), s32[]{:S(2)}) async-start(), calls=%async_computation.4 | async-start | bytes 7340032 | tf_op jit(solution)/shard_map/psum | solution.py:56
  170.9 214.5 %reduce-scatter.2.cloned.1.call-start = ((), (), s32[]{:S(2)}) async-start(), calls=%async_computation.6 | async-start | bytes 4456448 | tf_op jit(solution)/shard_map/reduce_scatter | solution.py:59
Sparse Core Ops, SparseCore 0:
  9.5 46.3 all-gather.6
  58.0 52.1 all-gather.8
  112.2 51.4 all-gather.4
  165.6 51.3 all-gather.10
  219.3 93.0 all-reduce.1
  320.2 65.1 reduce-scatter.1
where the time goes:
time: 394 us
  waiting for transfers between devices  353 us (90%)
  matrix products  23.4 us (6%)
  between operations  13.5 us (3%)
  other arithmetic  4 us (1%)
    psum x1, waiting for transfers between devices, on_device(): total = lax.psum(both, 'depth')  95.3 us
    reduce_scatter x1, waiting for transfers between devices, on_device(): lax.psum_scatter(jnp.dot(hidden, down_block, preferred_element_type=jnp.f...  65.3 us
    all_gather x1, waiting for transfers between devices, on_device(): up = add_one(lax.all_gather(up_masked, 'row', axis=0, tiled=True))  54.2 us
    all_gather x1, waiting for transfers between devices, on_device(): gate = add_one(lax.all_gather(gate_masked, 'row', axis=0, tiled=True))  48.7 us
    all_gather x1, waiting for transfers between devices, on_device(): down_block = lax.all_gather(down_masked, 'row', axis=0, tiled=True)  46.2 us
    all_gather x1, waiting for transfers between devices, on_device(): token_block = lax.all_gather(tokens, 'col', axis=0, tiled=True)  42.2 us
    dot_general x2, matrix products, add_panel(): return jnp.dot(token_block, piece, preferred_element_type=jnp.float32)  9.61 us
  transfers between devices with their start and end apart: 6, of which 6 were waited for; matrix products, arithmetic and copies ran while one was open for 5% of the time, Pallas kernels for 0%

commit v1 on v0

--- a/solution.py
+++ b/solution.py
@@ -2,6 +2,7 @@
 import jax.numpy as jnp
 from jax import lax
 from jax.sharding import PartitionSpec as P
+from jax.lax import all_to_all, psum
 
 BLOCK = 128
 
@@ -45,7 +46,9 @@
     down_masked = down_weight * keep_table(
         down_keep, down_start, depth_pos * down_features, down_rows_count, down_features
     )
-    token_block = lax.all_gather(tokens, "col", axis=0, tiled=True)
+    token_block = jnp.concatenate(
+        all_to_all(jnp.stack([tokens for _ in range(psum(1, "col"))], 0), "col", 0, 0), axis=0
+    )
 
     def add_one(piece):
         return add_panel(token_block, piece)

time: 394 us -> 351 us (0.89)
  the two profiles are of different devices: /device:TPU:25 before, /device:TPU:31 now
where the time goes in v1:
time: 351 us
  waiting for transfers between devices  254 us (72%)
  blocking collectives  56.1 us (16%)
  matrix products  23.5 us (7%)
  between operations  13.2 us (4%)
  other arithmetic  3.95 us (1%)
    psum x1, waiting for transfers between devices, on_device(): total = lax.psum(both, 'depth')  93.5 us
    reduce_scatter x1, waiting for transfers between devices, on_device(): lax.psum_scatter(jnp.dot(hidden, down_block, preferred_element_type=jnp.f...  67.4 us
    all_to_all x1, blocking collectives, on_device(): all_to_all(jnp.stack([tokens for _ in range(psum(1, 'col'))], 0), 'col',...  56.1 us
    all_gather x1, waiting for transfers between devices, on_device(): down_block = lax.all_gather(down_masked, 'row', axis=0, tiled=True)  46.9 us
    all_gather x1, waiting for transfers between devices, on_device(): gate = add_one(lax.all_gather(gate_masked, 'row', axis=0, tiled=True))  45.7 us
    dot_general x2, matrix products, add_panel(): return jnp.dot(token_block, piece, preferred_element_type=jnp.float32)  9.76 us
    dot_general x1, matrix products, on_device(): jnp.dot(hidden, down_block, preferred_element_type=jnp.float32)  7.61 us
  transfers between devices with their start and end apart: 5, of which 4 were waited for; matrix products, arithmetic and copies ran while one was open for 5% of the time, Pallas kernels for 0%

profile of v1, /device:TPU:31, one launch (start us, length us, event | category | flops | bytes accessed | tf_op | source)
XLA Modules:
  0.0 350.8 jit_solution(8787106681206974614)
XLA Ops:
  6.6 0.0 copy-start.2
  6.6 2.4 fusion.4
  9.0 0.0 all-gather.6.cloned.1.call-update
  9.0 0.0 all-gather.4.cloned.1.call-start
  9.1 2.3 fusion.3
  11.4 0.0 all-gather.4.cloned.1.call-update
  11.4 0.0 all-gather.8.cloned.1.call-start
  11.5 1.4 fusion
  13.0 0.0 all-gather.8.cloned.1.call-update
  13.0 0.0 all-reduce.2.cloned.1.call-start
  13.1 0.2 stack.8
  13.3 56.1 %all_to_all.5 = bf16[16,32,2048]{2,1,0:T(8,128)(2,1)S(1)} all-to-all(bf16[16,32,2048]{2,1,0:T(8,128)(2,1)S(1)} %stack.8), channel_id=1, replica_groups=mesh['row'=8,'col'=16,'depth'=4] {'col'}, dimensions={0} | all-to-all | bytes 4194304 | tf_op jit(solution)/shard_map/all_to_all | solution.py:50
  69.4 5.5 %convolution_bitcast_fusion = f32[1,512,896]{1,2,0:T(8,128)} fusion(bf16[2048,896]{1,0:T(8,128)(2,1)} %all-gather.6.cloned.1.call-done, bf16[512,2048]{1,0:T(8,128)(2,1)S(1)} %bitcast.26), kind=kOutput, calls=%fused_computation.8 | convolution fusion | flops 1879048192 | bytes 7602176 | tf_op jit(solution)/shard_map/dot_general | solution.py:25
  74.9 45.7 %all-gather.4.cloned.1.call-done = bf16[2048,896]{1,0:T(8,128)(2,1)} async-done(((bf16[256,896]{1,0:T(8,128)(2,1)}), bf16[2048,896]{1,0:T(8,128)(2,1)}) %all-gather.4.cloned.1.call-update) | async-done | bytes 3670032 | tf_op jit(solution)/shard_map/all_gather | solution.py:56
  120.7 4.3 %convolution_bitcast_fusion.1 = f32[1,512,896]{1,2,0:T(8,128)S(1)} fusion(bf16[2048,896]{1,0:T(8,128)(2,1)} %all-gather.4.cloned.1.call-done, bf16[512,2048]{1,0:T(8,128)(2,1)S(1)} %bitcast.27), kind=kOutput, calls=%fused_computation.9 | convolution fusion | flops 1879048192 | bytes 7602176 | tf_op jit(solution)/shard_map/dot_general | solution.py:25
  124.9 2.3 pad_maximum_fusion
  127.2 0.0 all-reduce.2.cloned.1.call-update
  127.3 0.0 reduce-scatter.2.cloned.1.call-start
  127.3 46.9 %all-gather.8.cloned.1.call-done = bf16[896,2048]{1,0:T(8,128)(2,1)} async-done(((bf16[112,2048]{1,0:T(8,128)(2,1)}), bf16[896,2048]{1,0:T(8,128)(2,1)}) %all-gather.8.cloned.1.call-update) | async-done | bytes 3670032 | tf_op jit(solution)/shard_map/all_gather | solution.py:61
  174.2 93.5 %all-reduce.2.cloned.1.call-done = f32[2,512,896]{1,2,0:T(8,128)} async-done(((f32[2,512,896]{1,2,0:T(8,128)}), f32[2,512,896]{1,2,0:T(8,128)}) %all-reduce.2.cloned.1.call-update) | async-done | bytes 3670032 | tf_op jit(solution)/shard_map/psum | solution.py:59
  267.7 7.6 %fusion.5 = f32[512,2048]{1,0:T(8,128)} fusion(bf16[896,2048]{1,0:T(8,128)(2,1)} %all-gather.8.cloned.1.call-done, f32[2,512,896]{1,2,0:T(8,128)} %all-reduce.2.cloned.1.call-done), kind=kOutput, calls=%fused_computation.16 | convolution fusion | flops 1881800704 | bytes 11534336 | tf_op jit(solution)/shard_map/dot_general | solution.py:63
  275.3 0.0 reduce-scatter.2.cloned.1.call-update
  275.3 67.4 %reduce-scatter.2.cloned.1.call-done = f32[32,2048]{1,0:T(8,128)} async-done(((f32[512,2048]{1,0:T(8,128)}), f32[32,2048]{1,0:T(8,128)}) %reduce-scatter.2.cloned.1.call-update) | async-done | bytes 262160 | tf_op jit(solution)/shard_map/reduce_scatter | solution.py:62
  342.6 1.6 convert_element_type.52
  (13 shorter events, 0.1 us)
Async XLA Ops:
  6.5 5.0 %copy-start.1 = (bf16[112,2048]{1,0:T(8,128)(2,1)S(1)}, bf16[112,2048]{1,0:T(8,128)(2,1)}, u32[]{:S(2)}) copy-start(bf16[112,2048]{1,0:T(8,128)(2,1)} %param.10) | copy-start | bytes 1376260
  6.5 5.0 %copy-start.3 = (s32[112,64]{0,1:T(8,128)S(1)}, s32[112,64]{0,1:T(8,128)}, u32[]{:S(2)}) copy-start(s32[112,64]{0,1:T(8,128)} %param.13) | copy-start | bytes 86020
  6.5 62.9 %all-gather.6.cloned.1.call-start = ((), (), s32[]{:S(2)}) async-start(), calls=%async_computation.3 | async-start | bytes 4128768 | tf_op jit(solution)/shard_map/all_gather | solution.py:57
  6.6 6.5 %copy-start.2 = (bf16[32,2048]{1,0:T(8,128)(2,1)S(1)}, bf16[32,2048]{1,0:T(8,128)(2,1)}, u32[]{:S(2)}) copy-start(bf16[32,2048]{1,0:T(8,128)(2,1)} %param.7) | copy-start | bytes 393220
  9.0 111.6 %all-gather.4.cloned.1.call-start = ((), (), s32[]{:S(2)}) async-start(), calls=%async_computation.2 | async-start | bytes 4128768 | tf_op jit(solution)/shard_map/all_gather | solution.py:56
  11.4 162.8 %all-gather.8.cloned.1.call-start = ((), (), s32[]{:S(2)}) async-start(), calls=%async_computation.5 | async-start | bytes 4128768 | tf_op jit(solution)/shard_map/all_gather | solution.py:61
  13.0 254.7 %all-reduce.2.cloned.1.call-start = ((), (), s32[]{:S(2)}) async-start(), calls=%async_computation.4 | async-start | bytes 7340032 | tf_op jit(solution)/shard_map/psum | solution.py:59
  120.7 4.3 %copy-start = (f32[1,512,896]{1,2,0:T(8,128)S(1)}, f32[1,512,896]{1,2,0:T(8,128)}, u32[]{:S(2)}) copy-start(f32[1,512,896]{1,2,0:T(8,128)} %convolution_bitcast_fusion) | copy-start | bytes 5505028
  127.3 215.4 %reduce-scatter.2.cloned.1.call-start = ((), (), s32[]{:S(2)}) async-start(), calls=%async_computation.6 | async-start | bytes 4456448 | tf_op jit(solution)/shard_map/reduce_scatter | solution.py:62
Sparse Core Ops, SparseCore 0:
  9.4 57.6 all-gather.5
  69.2 51.3 all-gather.3
  122.7 51.3 all-gather.7
  176.4 91.2 all-reduce.1
  275.4 67.1 reduce-scatter.1
